TPU v7x, 32 devices: a whole 2x2x4 slice. The times are simulated.
32 devices in a mesh: grp: 2 (over x), ta: 16 (over z, y, core).
Axes of the slice: x: 2, y: 2, z: 4, core: 2. Of those that a mesh axis runs over, the one named last changes fastest.
Arguments:
- frames_in: bfloat16 [32, 16, 128, 256], P(('grp', 'ta')), parts along dimension 0, may hold values from -6 to 6
- cotangent: bfloat16 [32, 16, 128, 256], P(('grp', 'ta')), parts along dimension 0, may hold values from -6 to 6
- spatial_w: bfloat16 [3, 3, 256, 256], replicated, may hold values from -0.125 to 0.125
- temporal_w: bfloat16 [3, 256, 256], replicated, may hold values from -0.21875 to 0.21875
Outputs:
- input_grad: bfloat16 [32, 16, 128, 256], P(('grp', 'ta')), parts along dimension 0
- spatial_grad: float32 [4608, 256], P(('grp', 'ta')), parts along dimension 0
- temporal_grad: float32 [1536, 256], P(('grp', 'ta')), parts along dimension 0
There are 2 independent parts, one for each index of `grp`. A program takes and returns all parts, laid end to end along the dimension named above; an argument that names none is the same for every part. Nothing has to cross between parts.
All inputs are finite; a program needn't handle non-finite values.
Results may differ from a plain program's by a relative error of at most 0.0031.
Values may be sent and summed in bfloat16 or wider, within the bound.
A program may use at most 64 MiB of HBM per device.

v0:
```python
import math

import jax
import jax.numpy as jnp
from jax import lax
from jax.sharding import PartitionSpec as P

TAP_DILATION = 1


def shifted(value, axis, by):
    size = lax.axis_size(axis)
    pairs = [(i, i + by) for i in range(size) if 0 <= i + by < size]
    return lax.ppermute(value, axis, pairs)


def body(frames_in, cotangent, spatial_w, temporal_w):
    resident_frames, rows, cols, chans = frames_in.shape
    devices = lax.axis_size("ta")
    shift_count = TAP_DILATION // resident_frames
    g_scale = 1.0 / math.sqrt(resident_frames * devices * rows * cols)
    earlier = [frames_in]
    for tap_number in (1, 2):
        earlier.append(shifted(frames_in, "ta", tap_number * shift_count))
    preactivation = jnp.einsum(
        "fhwc,cd->fhwd", earlier[0], temporal_w[0], preferred_element_type=jnp.float32
    )
    for tap_number in (1, 2):
        preactivation = preactivation + jnp.einsum(
            "fhwc,cd->fhwd",
            earlier[tap_number],
            temporal_w[tap_number],
            preferred_element_type=jnp.float32,
        )
    act = jax.nn.silu(preactivation).astype(jnp.bfloat16)
    up_pad = jnp.pad(cotangent, ((0, 0), (1, 1), (1, 1), (0, 0)))
    act_pad = jnp.pad(act, ((0, 0), (1, 1), (1, 1), (0, 0)))
    act_grad = jnp.zeros(preactivation.shape, jnp.float32)
    blocks = []
    for row_i in range(3):
        for col_j in range(3):
            piece = up_pad[:, 2 - row_i : 2 - row_i + rows, 2 - col_j : 2 - col_j + cols]
            act_grad = act_grad + jnp.einsum(
                "fhwd,cd->fhwc", piece, spatial_w[row_i, col_j], preferred_element_type=jnp.float32
            )
            moved = act_pad[:, row_i : row_i + rows, col_j : col_j + cols]
            blocks.append(
                jnp.einsum("fhwc,fhwd->cd", moved, cotangent, preferred_element_type=jnp.float32)
            )
    spatial_term = jnp.concatenate(blocks, axis=0)
    spatial_grad = lax.psum_scatter(spatial_term, "ta", scatter_dimension=0, tiled=True) * g_scale
    sigmoid_v = jax.nn.sigmoid(preactivation)
    v_grad = (act_grad * sigmoid_v * (1.0 + preactivation * (1.0 - sigmoid_v))).astype(jnp.bfloat16)
    later = [v_grad]
    for tap_number in (1, 2):
        later.append(shifted(v_grad, "ta", -tap_number * shift_count))
    temporal_layers = []
    temporal_adjoint = jnp.zeros(preactivation.shape, jnp.float32)
    for tap_number in range(3):
        temporal_layers.append(
            jnp.einsum(
                "fhwc,fhwd->cd", earlier[tap_number], v_grad, preferred_element_type=jnp.float32
            )
        )
        temporal_adjoint = temporal_adjoint + jnp.einsum(
            "fhwd,cd->fhwc",
            later[tap_number],
            temporal_w[tap_number],
            preferred_element_type=jnp.float32,
        )
    temporal_term = jnp.concatenate(temporal_layers, axis=0)
    temporal_grad = lax.psum_scatter(temporal_term, "ta", scatter_dimension=0, tiled=True) * g_scale
    input_grad = (cotangent.astype(jnp.float32) + temporal_adjoint).astype(jnp.bfloat16)
    return (input_grad, spatial_grad, temporal_grad)


def solution(mesh):
    in_specs = (P(("grp", "ta"), None, None, None), P(("grp", "ta"), None, None, None), P(), P())
    out_specs = (P(("grp", "ta"), None, None, None), P(("grp", "ta"), None), P(("grp", "ta"), None))
    return jax.shard_map(body, mesh=mesh, in_specs=in_specs, out_specs=out_specs, check_vma=False)
```

profile of v0, /device:TPU:0, one launch (start us, length us, event | category | flops | bytes accessed | tf_op | source)
XLA Modules:
  0.0 194.8 jit_solution(3913523184359245802)
XLA Ops:
  7.2 0.0 copy-start.4
  7.2 0.0 reduce-scatter.5.cloned.1.call-start
  7.2 2.6 %collective-permute-start = (bf16[1,16,128,256]{3,2,1,0:T(8,128)(2,1)}, bf16[1,16,128,256]{3,2,1,0:T(8,128)(2,1)S(1)}, u32[]{:S(2)}, u32[]{:S(2)}) collective-permute-start(bf16[1,16,128,256]{3,2,1,0:T(8,128)(2,1)} %param.4), channel_id=1, source_target_pairs={{0,1},{1,2},{2,3},{3,4},{4,5},{5,6},{6,7},{7,8},{8,9},{9,10},{10,1... | collective-permute-start | bytes 3145736 | tf_op jit(solution)/shard_map/ppermute | solution.py:14
  9.8 4.4 %collective-permute-start.1 = (bf16[1,16,128,256]{3,2,1,0:T(8,128)(2,1)}, bf16[1,16,128,256]{3,2,1,0:T(8,128)(2,1)S(1)}, u32[]{:S(2)}, u32[]{:S(2)}) collective-permute-start(bf16[1,16,128,256]{3,2,1,0:T(8,128)(2,1)} %param.4), channel_id=1, source_target_pairs={{0,2},{1,3},{2,4},{3,5},{4,6},{5,7},{6,8},{7,9},{8,10},{9,11},{10,... | collective-permute-start | bytes 3145736 | tf_op jit(solution)/shard_map/ppermute | solution.py:14
  14.2 1.7 fusion.30
  15.9 0.5 fusion.32
  16.4 0.5 fusion.34
  16.9 0.5 fusion.47
  17.4 0.5 fusion.49
  17.9 0.5 fusion.53
  18.4 0.5 fusion.51
  18.8 0.0 copy-start.3
  18.9 0.0 copy-start.5
  18.9 1.5 fusion.45
  20.4 0.4 fusion.27
  20.8 0.0 collective-permute-done
  20.8 0.4 fusion.24
  21.2 16.8 %collective-permute-done.1 = bf16[1,16,128,256]{3,2,1,0:T(8,128)(2,1)S(1)} collective-permute-done((bf16[1,16,128,256]{3,2,1,0:T(8,128)(2,1)}, bf16[1,16,128,256]{3,2,1,0:T(8,128)(2,1)S(1)}, u32[]{:S(2)}, u32[]{:S(2)}) %collective-permute-start.1) | collective-permute-done | bytes 1048608 | tf_op jit(solution)/shard_map/ppermute | solution.py:14
  38.1 0.5 add_add_fusion
  38.6 0.6 fusion.134
  39.2 0.5 fusion.9
  39.6 0.5 fusion.8
  40.1 0.5 fusion.7
  40.6 0.5 fusion.6
  41.1 2.7 %multiply_convert_fusion.1 = bf16[16,128,256]{2,1,0:T(8,128)(2,1)S(1)} fusion(f32[16,128,256]{2,1,0:T(8,128)S(1)} %add_add_fusion, f32[16,128,256]{2,1,0:T(8,128)S(1)} %fusion.30, f32[16,128,256]{2,1,0:T(8,128)S(1)} %fusion.32, f32[16,128,256]{2,1,0:T(8,128)S(1)} %fusion.34, f32[16,128,256]{2,1,0:T(8,128)S(1)} %fusion.45, f32[16,128,256]{2,1,0:T(8,128)S(1)} %fusion.47, ...), kind=kOutput, calls=%fused_computation.3 | convolution fusion | flops 277348352 | bytes 21102592 | tf_op jit(solution)/shard_map/fhwd,cd->fhwc/dot_general | solution.py:43
  43.9 0.5 convolution_bitcast_fusion.2
  44.4 0.5 convolution_bitcast_fusion
  45.0 0.5 convolution_bitcast_fusion.1
  45.5 0.9 pad_maximum_fusion
  46.4 0.0 reduce-scatter.5.cloned.1.call-update
  46.5 0.0 reduce-scatter.3.cloned.1.call-start
  46.5 3.0 %fusion.5 = f32[2304,256]{1,0:T(8,128)} fusion(f32[2304,256]{1,0:T(8,128)} %copy-done.2, bf16[1,16,128,256]{3,2,1,0:T(8,128)(2,1)S(1)} %copy-done, f32[16,128,256]{2,1,0:T(8,128)} %copy-done.1), kind=kOutput, calls=%fused_computation.18 | convolution fusion | flops 271056896 | bytes 3407872 | tf_op jit(solution)/shard_map/fhwc,fhwd->cd/dot_general | solution.py:48
  49.5 1.2 fusion.4
  50.7 1.2 fusion.3
  51.9 1.2 fusion.2
  53.1 1.2 fusion.1
  54.3 0.0 reduce-scatter.3.cloned.1.call-update
  54.3 1.3 collective-permute-start.2
  55.6 1.3 collective-permute-start.3
  56.9 0.5 fusion.100
  57.4 9.8 %collective-permute-done.2 = bf16[1,16,128,256]{3,2,1,0:T(8,128)(2,1)S(1)} collective-permute-done((bf16[1,16,128,256]{3,2,1,0:T(8,128)(2,1)S(1)}, bf16[1,16,128,256]{3,2,1,0:T(8,128)(2,1)S(1)}, u32[]{:S(2)}, u32[]{:S(2)}) %collective-permute-start.2) | collective-permute-done | bytes 1048608 | tf_op jit(solution)/shard_map/ppermute | solution.py:14
  67.2 0.5 fusion.19
  67.6 36.4 %collective-permute-done.3 = bf16[1,16,128,256]{3,2,1,0:T(8,128)(2,1)S(1)} collective-permute-done((bf16[1,16,128,256]{3,2,1,0:T(8,128)(2,1)S(1)}, bf16[1,16,128,256]{3,2,1,0:T(8,128)(2,1)S(1)}, u32[]{:S(2)}, u32[]{:S(2)}) %collective-permute-start.3) | collective-permute-done | bytes 1048608 | tf_op jit(solution)/shard_map/ppermute | solution.py:14
  104.0 1.7 fusion
  105.7 14.4 %reduce-scatter.5.cloned.1.call-done = f32[48,256]{1,0:T(8,128)} async-done(((f32[768,256]{1,0:T(8,128)}), f32[48,256]{1,0:T(8,128)}) %reduce-scatter.5.cloned.1.call-update) | async-done | bytes 49168 | tf_op jit(solution)/shard_map/reduce_scatter | solution.py:72
  120.1 1.4 broadcast_multiply_fusion.1
  121.5 64.9 %reduce-scatter.3.cloned.1.call-done = f32[144,256]{1,0:T(8,128)} async-done(((f32[2304,256]{1,0:T(8,128)}), f32[144,256]{1,0:T(8,128)}) %reduce-scatter.3.cloned.1.call-update) | async-done | bytes 147472 | tf_op jit(solution)/shard_map/reduce_scatter | solution.py:51
  186.4 1.6 broadcast_multiply_fusion
  (9 shorter events, 0.0 us)
Async XLA Ops:
  7.2 8.8 %copy-start = (bf16[1,16,128,256]{3,2,1,0:T(8,128)(2,1)S(1)}, bf16[1,16,128,256]{3,2,1,0:T(8,128)(2,1)}, u32[]{:S(2)}) copy-start(bf16[1,16,128,256]{3,2,1,0:T(8,128)(2,1)} %param.5) | copy-start | bytes 3145732
  7.2 8.8 %copy-start.4 = (bf16[3,3,256,256]{3,2,1,0:T(8,128)(2,1)S(1)}, bf16[3,3,256,256]{3,2,1,0:T(8,128)(2,1)}, u32[]{:S(2)}) copy-start(bf16[3,3,256,256]{3,2,1,0:T(8,128)(2,1)} %param.6) | copy-start | bytes 3538948
  7.2 112.9 %reduce-scatter.5.cloned.1.call-start = ((), (), s32[]{:S(2)}) async-start(), calls=%async_computation.3 | async-start | bytes 835584 | tf_op jit(solution)/shard_map/reduce_scatter | solution.py:72
  7.2 13.6 %collective-permute-start = (bf16[1,16,128,256]{3,2,1,0:T(8,128)(2,1)}, bf16[1,16,128,256]{3,2,1,0:T(8,128)(2,1)S(1)}, u32[]{:S(2)}, u32[]{:S(2)}) collective-permute-start(bf16[1,16,128,256]{3,2,1,0:T(8,128)(2,1)} %param.4), channel_id=1, source_target_pairs={{0,1},{1,2},{2,3},{3,4},{4,5},{5,6},{6,7},{7,8},{8,9},{9,10},{10,1... | collective-permute-start | bytes 3145736 | tf_op jit(solution)/shard_map/ppermute | solution.py:14
  9.8 28.3 %collective-permute-start.1 = (bf16[1,16,128,256]{3,2,1,0:T(8,128)(2,1)}, bf16[1,16,128,256]{3,2,1,0:T(8,128)(2,1)S(1)}, u32[]{:S(2)}, u32[]{:S(2)}) collective-permute-start(bf16[1,16,128,256]{3,2,1,0:T(8,128)(2,1)} %param.4), channel_id=1, source_target_pairs={{0,2},{1,3},{2,4},{3,5},{4,6},{5,7},{6,8},{7,9},{8,10},{9,11},{10,... | collective-permute-start | bytes 3145736 | tf_op jit(solution)/shard_map/ppermute | solution.py:14
  18.8 1.5 copy-start.3
  18.9 1.5 copy-start.5
  38.6 2.5 %copy-start.1 = (f32[16,128,256]{2,1,0:T(8,128)}, f32[16,128,256]{2,1,0:T(8,128)S(1)}, u32[]{:S(2)}) copy-start(f32[16,128,256]{2,1,0:T(8,128)S(1)} %add_add_fusion) | copy-start | bytes 6291460
  41.1 2.8 %copy-start.2 = (f32[2304,256]{1,0:T(8,128)}, f32[2304,256]{1,0:T(8,128)S(1)}, u32[]{:S(2)}) copy-start(f32[2304,256]{1,0:T(8,128)S(1)} %fusion.6) | copy-start | bytes 7077892
  46.5 139.9 %reduce-scatter.3.cloned.1.call-start = ((), (), s32[]{:S(2)}) async-start(), calls=%async_computation.2 | async-start | bytes 2506752 | tf_op jit(solution)/shard_map/reduce_scatter | solution.py:51
  54.3 12.8 %collective-permute-start.2 = (bf16[1,16,128,256]{3,2,1,0:T(8,128)(2,1)S(1)}, bf16[1,16,128,256]{3,2,1,0:T(8,128)(2,1)S(1)}, u32[]{:S(2)}, u32[]{:S(2)}) collective-permute-start(bf16[1,16,128,256]{3,2,1,0:T(8,128)(2,1)S(1)} %bitcast.212), channel_id=1, source_target_pairs={{1,0},{2,1},{3,2},{4,3},{5,4},{6,5},{7,6},{8,7},{9,8},{10,9},{11,1... | collective-permute-start | bytes 3145736 | tf_op jit(solution)/shard_map/ppermute | solution.py:14
  55.6 48.4 %collective-permute-start.3 = (bf16[1,16,128,256]{3,2,1,0:T(8,128)(2,1)S(1)}, bf16[1,16,128,256]{3,2,1,0:T(8,128)(2,1)S(1)}, u32[]{:S(2)}, u32[]{:S(2)}) collective-permute-start(bf16[1,16,128,256]{3,2,1,0:T(8,128)(2,1)S(1)} %bitcast.213), channel_id=1, source_target_pairs={{2,0},{3,1},{4,2},{5,3},{6,4},{7,5},{8,6},{9,7},{10,8},{11,9},{12,... | collective-permute-start | bytes 3145736 | tf_op jit(solution)/shard_map/ppermute | solution.py:14
Sparse Core Ops, SparseCore 0:
  46.6 73.4 reduce-scatter.4
  124.3 62.0 reduce-scatter.2
where the time goes:
time: 195 us
  waiting for transfers between devices  142 us (73%)
  matrix products  24 us (12%)
  between operations  14.3 us (7%)
  starting transfers between devices  9.66 us (5%)
  other arithmetic  4.53 us (2%)
    reduce_scatter x1, waiting for transfers between devices, body(): lax.psum_scatter(spatial_term, 'ta', scatter_dimension=0, tiled=True)  64.9 us
    ppermute x4, waiting for transfers between devices, shifted(): return lax.ppermute(value, axis, pairs)  63 us
    reduce_scatter x1, waiting for transfers between devices, body(): lax.psum_scatter(temporal_term, 'ta', scatter_dimension=0, tiled=True)  14.4 us
    dot_general x9, matrix products, body(): jnp.einsum('fhwc,fhwd->cd', moved, cotangent, preferred_element_type=jnp....  9.7 us
    ppermute x4, starting transfers between devices, shifted(): return lax.ppermute(value, axis, pairs)  9.58 us
    dot_general x9, matrix products, body(): jnp.einsum('fhwd,cd->fhwc', piece, spatial_w[row_i, col_j], preferred_ele...  8.77 us
  transfers between devices with their start and end apart: 6, of which 5 were waited for; matrix products, arithmetic and copies ran while one was open for 10% of the time, Pallas kernels for 0%

commit v1 on v0

v1 whole, which is shorter than its diff:
```python
import functools
import math

import jax
import jax.numpy as jnp
from jax import lax
from jax.experimental import pallas as pl
from jax.experimental.pallas import tpu as pltpu
from jax.sharding import PartitionSpec as P

F32, BF16 = jnp.float32, jnp.bfloat16
CHUNKS = 4
LAG = 4


def dot(a, b):
    return jnp.dot(a, b, preferred_element_type=F32)


def dot_t(a, b):
    return lax.dot_general(a, b, (((1,), (1,)), ((), ())), preferred_element_type=F32)


def kernel(
    n, cells, cols, chans, fused, g_scale,
    x_hbm, cot_hbm, sw_hbm, tw_hbm, *rest,
):
    if fused:
        out_hbm, sg_hbm, tg_hbm = rest[:3]
    else:
        out_hbm, sg_hbm, tg_hbm = rest[:3]
    (cotp, sw, tw, xs, vgs, agrad, act_t, x_t, s_sum, t_sum, out_v,
     local_sem, out_sem, xsend, xfwd, xrecv, vsend, vfwd, vrecv) = rest[3:22]
    me = lax.axis_index("ta")
    core = lax.rem(me, 2)
    even = core == 0
    size = cells // CHUNKS

    def rows(k):
        return pl.ds(pl.multiple_of(k * size, size), size)

    def remote(src, dst, ssem, rsem, to):
        return pltpu.make_async_remote_copy(
            src_ref=src, dst_ref=dst, send_sem=ssem, recv_sem=rsem,
            device_id={"ta": to}, device_id_type=pl.DeviceIdType.MESH,
        )

    steps = [1, 2, n - 1, n - 2]
    if fused:
        steps += [4, 8, 12]
    barrier = pltpu.get_barrier_semaphore()
    for step in steps:
        pl.semaphore_signal(
            barrier, inc=1, device_id={"ta": lax.rem(me + step, n)},
            device_id_type=pl.DeviceIdType.MESH,
        )
    loads = [
        pltpu.make_async_copy(cot_hbm, cotp.at[1, pl.ds(cols, cells)], local_sem.at[0]),
        pltpu.make_async_copy(sw_hbm, sw, local_sem.at[1]),
        pltpu.make_async_copy(x_hbm, xs.at[0], local_sem.at[2]),
        pltpu.make_async_copy(tw_hbm, tw, local_sem.at[3]),
    ]
    for load in loads:
        load.start()
    pl.semaphore_wait(barrier, len(steps))

    def x_one(k):
        return remote(x_hbm.at[rows(k)], xs.at[1, rows(k)], xsend.at[0, k], xrecv.at[0, k],
                      lax.rem(me + 1, n))

    def x_two(k):
        return remote(x_hbm.at[rows(k)], xs.at[2, rows(k)], xsend.at[1, k], xrecv.at[1, k],
                      lax.rem(me + 2, n))

    def x_pass(k):
        return remote(xs.at[1, rows(k)], xs.at[2, rows(k)], xfwd.at[k], xrecv.at[1, k],
                      lax.rem(me + 1, n))

    def v_one(k):
        return remote(vgs.at[0, rows(k)], vgs.at[1, rows(k)], vsend.at[0, k], vrecv.at[0, k],
                      lax.rem(me + n - 1, n))

    def v_two(k):
        return remote(vgs.at[0, rows(k)], vgs.at[2, rows(k)], vsend.at[1, k], vrecv.at[1, k],
                      lax.rem(me + n - 2, n))

    def v_pass(k):
        return remote(vgs.at[1, rows(k)], vgs.at[2, rows(k)], vfwd.at[k], vrecv.at[1, k],
                      lax.rem(me + n - 1, n))

    x_has_one, x_has_two = me < n - 1, jnp.logical_and(even, me < n - 2)
    x_has_pass = jnp.logical_and(even, me >= 2)
    v_has_one, v_has_two = me >= 1, jnp.logical_and(core == 1, me >= 2)
    v_has_pass = jnp.logical_and(core == 1, me < n - 1)

    for k in range(CHUNKS):
        @pl.when(x_has_one)
        def _():
            x_one(k).start()

        @pl.when(x_has_two)
        def _():
            x_two(k).start()

    @pl.when(me == 0)
    def _():
        xs[1] = jnp.zeros((cells, chans), BF16)

    @pl.when(me < 2)
    def _():
        xs[2] = jnp.zeros((cells, chans), BF16)

    @pl.when(me == n - 1)
    def _():
        vgs[1] = jnp.zeros((cells, chans), BF16)

    @pl.when(me >= n - 2)
    def _():
        vgs[2] = jnp.zeros((cells, chans), BF16)

    edge = jnp.zeros((cols, chans), BF16)
    for j in range(3):
        cotp[j, pl.ds(0, cols)] = edge
        cotp[j, pl.ds(cols + cells, cols)] = edge
    loads[0].wait()

    def shift(k, carry):
        at = pl.ds(pl.multiple_of(cols + k * size, cols), size)
        piece = cotp[1, at].astype(F32)
        col = lax.rem(lax.broadcasted_iota(jnp.int32, (size, chans), 0), cols)
        cotp[0, at] = jnp.where(col == cols - 1, 0.0, pltpu.roll(piece, size - 1, 0)).astype(BF16)
        cotp[2, at] = jnp.where(col == 0, 0.0, pltpu.roll(piece, 1, 0)).astype(BF16)
        return carry

    lax.fori_loop(0, CHUNKS, shift, 0)
    loads[1].wait()

    def cot_at(k, i, j):
        return cotp[j, pl.ds(pl.multiple_of(k * size + (2 - i) * cols, cols), size)]

    def adjoint(k, carry):
        total = jnp.zeros((size, chans), F32)
        for i in range(3):
            for j in range(3):
                total = total + dot_t(cot_at(k, i, j), sw[i, j])
        agrad[rows(k)] = total
        return carry

    lax.fori_loop(0, CHUNKS, adjoint, 0)
    loads[2].wait()
    loads[3].wait()
    s_sum[...] = jnp.zeros_like(s_sum)
    t_sum[...] = jnp.zeros_like(t_sum)

    def send_v(k):
        @pl.when(v_has_one)
        def _():
            v_one(k).start()

        @pl.when(v_has_two)
        def _():
            v_two(k).start()

    def forward(k, carry):
        @pl.when(me >= 1)
        def _():
            x_one(k).wait_recv()

        @pl.when(x_has_pass)
        def _():
            x_pass(k).start()

        @pl.when(me >= 2)
        def _():
            x_two(k).wait_recv()

        at = rows(k)
        v = dot(xs[0, at], tw[0]) + dot(xs[1, at], tw[1]) + dot(xs[2, at], tw[2])
        s = 1.0 / (1.0 + jnp.exp(-v))
        vg = (agrad[at] * s * (1.0 + v * (1.0 - s))).astype(BF16)
        vgs[0, at] = vg
        act_t[...] = (v * s).astype(BF16).T
        if LAG < CHUNKS:
            @pl.when(k >= LAG)
            def _():
                send_v(k - LAG)
        for tap in range(3):
            x_t[tap * chans : (tap + 1) * chans] = xs[tap, at].T
        t_sum[...] += dot(x_t[...], vgs[0, at])
        for i in range(3):
            for j in range(3):
                block = pl.ds((3 * i + j) * chans, chans)
                s_sum[block] += dot(act_t[...], cot_at(k, i, j))
        return carry

    lax.fori_loop(0, CHUNKS, forward, 0)
    for k in range(max(CHUNKS - LAG, 0), CHUNKS):
        send_v(k)

    def back(k):
        @pl.when(me < n - 1)
        def _():
            v_one(k).wait_recv()

        @pl.when(v_has_pass)
        def _():
            v_pass(k).start()

        at = rows(k)
        total = dot_t(vgs[0, at], tw[0]) + dot_t(vgs[1, at], tw[1])

        @pl.when(me < n - 2)
        def _():
            v_two(k).wait_recv()

        total = total + dot_t(vgs[2, at], tw[2])
        cot = cotp[1, pl.ds(pl.multiple_of(cols + k * size, cols), size)].astype(F32)
        out_v[at] = (cot + total).astype(BF16)
        pltpu.make_async_copy(out_v.at[at], out_hbm.at[at], out_sem.at[k]).start()

    if fused:
        (send1, recv1, send2, recv2, send3, recv3, sg, tg,
         sem1, rsem1, sem2, rsem2, sem3, rsem3) = rest[22:]
        z = me // 4
        y = lax.rem(me // 2, 2)
        sr = 9 * chans // n
        tr = 3 * chans // n

        def own(b):
            return (s_sum[pl.ds(pl.multiple_of(sr * b, 16), sr)],
                    t_sum[pl.ds(pl.multiple_of(tr * b, 16), tr)])

        stage1 = []
        for part in range(2):
            to_y = 1 - y if part == 0 else y
            for zz in range(4):
                a, b = own(4 * zz + 2 * to_y + (1 - core))
                send1[part, zz, 0:sr] = a.astype(BF16)
                send1[part, zz, sr : sr + tr] = b.astype(BF16)
            copy = remote(send1.at[part], recv1.at[part], sem1.at[part], rsem1.at[part],
                          me + 1 - 2 * core)
            copy.start()
            stage1.append(copy)
        stage1[0].wait_recv()
        for zz in range(4):
            a, b = own(4 * zz + 2 * (1 - y) + core)
            send2[zz, 0:sr] = (a + recv1[0, zz, 0:sr].astype(F32)).astype(BF16)
            send2[zz, sr : sr + tr] = (b + recv1[0, zz, sr : sr + tr].astype(F32)).astype(BF16)
        stage2 = remote(send2, recv2, sem2.at[0], rsem2.at[0], me + 2 - 4 * y)
        stage2.start()
        half = CHUNKS // 2
        for k in range(half):
            back(k)
        stage1[1].wait_recv()
        stage2.wait_recv()

        def sum2(zz):
            a, b = own(4 * zz + 2 * y + core)
            a = a + recv1[1, zz, 0:sr].astype(F32) + recv2[zz, 0:sr].astype(F32)
            b = (b + recv1[1, zz, sr : sr + tr].astype(F32)
                 + recv2[zz, sr : sr + tr].astype(F32))
            return a, b

        stage3 = []
        for dz in (2, 1, 3):
            zz = lax.rem(z + dz, 4)
            a, b = sum2(zz)
            send3[dz - 1, 0:sr] = a.astype(BF16)
            send3[dz - 1, sr : sr + tr] = b.astype(BF16)
            copy = remote(send3.at[dz - 1], recv3.at[dz - 1], sem3.at[dz - 1], rsem3.at[dz - 1],
                          lax.rem(me + 4 * dz, n))
            copy.start()
            stage3.append(copy)
        for k in range(half, CHUNKS):
            back(k)
        a, b = sum2(z)
        for copy in stage3:
            copy.wait_recv()
        for slot in range(3):
            a = a + recv3[slot, 0:sr].astype(F32)
            b = b + recv3[slot, sr : sr + tr].astype(F32)
        sg[...] = a * g_scale
        tg[...] = b * g_scale
        ends = [pltpu.make_async_copy(sg, sg_hbm, local_sem.at[0]),
                pltpu.make_async_copy(tg, tg_hbm, local_sem.at[1])]
        for copy in ends:
            copy.start()
        for copy in stage1 + [stage2] + stage3:
            copy.wait_send()
    else:
        ends = [pltpu.make_async_copy(s_sum, sg_hbm, local_sem.at[0]),
                pltpu.make_async_copy(t_sum, tg_hbm, local_sem.at[1])]
        for copy in ends:
            copy.start()
        for k in range(CHUNKS):
            back(k)

    for k in range(CHUNKS):
        for has, copy in ((x_has_one, x_one), (x_has_two, x_two), (x_has_pass, x_pass),
                          (v_has_one, v_one), (v_has_two, v_two), (v_has_pass, v_pass)):
            @pl.when(has)
            def _():
                copy(k).wait_send()
        pltpu.make_async_copy(out_v.at[rows(k)], out_hbm.at[rows(k)], out_sem.at[k]).wait()
    for copy in ends:
        copy.wait()


def body(n, frames_in, cotangent, spatial_w, temporal_w):
    resident, height, cols, chans = frames_in.shape
    cells = resident * height * cols
    g_scale = 1.0 / math.sqrt(n * cells)
    sr, tr = 9 * chans // n, 3 * chans // n
    fused = n == 16 and sr % 16 == 0 and tr % 16 == 0
    both = sr + tr
    dma = pltpu.SemaphoreType.DMA
    scratch = [
        pltpu.VMEM((3, cells + 2 * cols, chans), BF16),
        pltpu.VMEM((3, 3, chans, chans), BF16),
        pltpu.VMEM((3, chans, chans), BF16),
        pltpu.VMEM((3, cells, chans), BF16),
        pltpu.VMEM((3, cells, chans), BF16),
        pltpu.VMEM((cells, chans), F32),
        pltpu.VMEM((chans, cells // CHUNKS), BF16),
        pltpu.VMEM((3 * chans, cells // CHUNKS), BF16),
        pltpu.VMEM((9 * chans, chans), F32),
        pltpu.VMEM((3 * chans, chans), F32),
        pltpu.VMEM((cells, chans), BF16),
        dma((4,)), dma((CHUNKS,)),
        dma((2, CHUNKS)), dma((CHUNKS,)), dma((2, CHUNKS)),
        dma((2, CHUNKS)), dma((CHUNKS,)), dma((2, CHUNKS)),
    ]
    if fused:
        scratch += [
            pltpu.VMEM((2, 4, both, chans), BF16), pltpu.VMEM((2, 4, both, chans), BF16),
            pltpu.VMEM((4, both, chans), BF16), pltpu.VMEM((4, both, chans), BF16),
            pltpu.VMEM((3, both, chans), BF16), pltpu.VMEM((3, both, chans), BF16),
            pltpu.VMEM((sr, chans), F32), pltpu.VMEM((tr, chans), F32),
            dma((2,)), dma((2,)), dma((1,)), dma((1,)), dma((3,)), dma((3,)),
        ]
    else:
        sr, tr = 9 * chans, 3 * chans
    anywhere = pl.BlockSpec(memory_space=pl.ANY)
    input_grad, sg, tg = pl.pallas_call(
        functools.partial(kernel, n, cells, cols, chans, fused, g_scale),
        out_shape=(
            jax.ShapeDtypeStruct((cells, chans), BF16),
            jax.ShapeDtypeStruct((sr, chans), F32),
            jax.ShapeDtypeStruct((tr, chans), F32),
        ),
        in_specs=[anywhere] * 4,
        out_specs=(anywhere,) * 3,
        scratch_shapes=scratch,
        compiler_params=pltpu.CompilerParams(
            collective_id=0, has_side_effects=True, vmem_limit_bytes=56 * 1024 * 1024
        ),
    )(frames_in.reshape(cells, chans), cotangent.reshape(cells, chans), spatial_w, temporal_w)
    if not fused:
        sg = lax.psum_scatter(sg, "ta", scatter_dimension=0, tiled=True) * g_scale
        tg = lax.psum_scatter(tg, "ta", scatter_dimension=0, tiled=True) * g_scale
    return input_grad.reshape(frames_in.shape), sg, tg


def solution(mesh):
    n = mesh.shape["ta"]
    in_specs = (P(("grp", "ta"), None, None, None), P(("grp", "ta"), None, None, None), P(), P())
    out_specs = (P(("grp", "ta"), None, None, None), P(("grp", "ta"), None), P(("grp", "ta"), None))
    return jax.shard_map(
        functools.partial(body, n), mesh=mesh, in_specs=in_specs, out_specs=out_specs,
        check_vma=False,
    )
```

time: 195 us -> 78.6 us (0.40)
  waiting for transfers between devices: 142 us -> 0 us
  Pallas kernels: 0 us -> 74.1 us
  matrix products: 24 us -> 0 us
  between operations: 14.3 us -> 0.66 us
  starting transfers between devices: 9.66 us -> 0 us
  other arithmetic: 4.53 us -> 0 us
  local copies, waits for them, and re-layouts: 0.03 us -> 3.61 us
    reduce_scatter x2 -> x0, waiting for transfers between devices: 79.3 us -> none  [the longest x1 64.9 us: body(): lax.psum_scatter(spatial_term, 'ta', scatter_dimension=0, tiled=True)]
    pallas_call x0 -> x1, Pallas kernels: none -> 74.1 us  [body(): pl.pallas_call(functools.partial(kernel, n, cells, cols, chans, fused, g_...]
    ppermute x4 -> x0, waiting for transfers between devices: 63 us -> none  [shifted(): return lax.ppermute(value, axis, pairs)]
    dot_general x27 -> x0, matrix products: 24 us -> none  [the longest x9 9.7 us: body(): jnp.einsum('fhwc,fhwd->cd', moved, cotangent, preferred_element_type=jnp....]
    ppermute x4 -> x0, starting transfers between devices: 9.58 us -> none  [shifted(): return lax.ppermute(value, axis, pairs)]
    unnamed x12 -> x7, local copies, waits for them, and re-layouts: 0.03 us -> 3.61 us
    mul x2 -> x0, other arithmetic: 3.01 us -> none  [the longest x1 1.58 us: body(): lax.psum_scatter(spatial_term, 'ta', scatter_dimension=0, tiled=True)]
  transfers between devices with their start and end apart: 6 -> 0, of which waited for: 5 -> 0; matrix products, arithmetic and copies ran while one was open for 10% -> 0% of each run, Pallas kernels for 0% -> 0%
where the time goes in v1:
time: 78.6 us; the launch traced here: 78.4 us
  Pallas kernels  74.1 us (94%)
  local copies, waits for them, and re-layouts  3.61 us (5%)
    pallas_call x1, Pallas kernels, body(): pl.pallas_call(functools.partial(kernel, n, cells, cols, chans, fused, g_...  74.1 us
    unnamed x7, local copies, waits for them, and re-layouts  3.61 us

profile of v1, /device:TPU:0, one launch (start us, length us, event | category | flops | bytes accessed | tf_op | source)
XLA Modules:
  0.0 78.4 jit_solution(6179078464152299188)
XLA Ops:
  0.6 74.1 %shard_map.67 = (bf16[2048,256]{1,0:T(8,128)(2,1)}, f32[144,256]{1,0:T(8,128)}, f32[48,256]{1,0:T(8,128)}) custom-call(bf16[2048,256]{1,0:T(8,128)(2,1)} %bitcast.3, bf16[2048,256]{1,0:T(8,128)(2,1)} %bitcast.4, bf16[3,3,256,256]{3,2,1,0:T(8,128)(2,1)} %sw_hbm.1, bf16[3,256,256]{2,1,0:T(8,128)(2,1)} %tw_hbm.1), custom_call_target="tpu_custom_call" | custom-call | tf_op jit(solution)/shard_map/pallas_call | solution.py:344
  74.8 0.0 copy-start
  74.8 0.0 copy-start.1
  74.8 2.3 %copy.10 = bf16[1,16,128,256]{3,2,1,0:T(8,128)(2,1)} copy(bf16[1,16,128,256]{3,2,1,0:T(8,128)(2,1)} %bitcast.5) | data formatting | bytes 2097152
  77.1 0.0 copy-done
  77.1 0.7 copy.11
  77.8 0.0 copy-done.1
  77.8 0.6 copy.12
Async XLA Ops:
  74.8 2.3 %copy-start = (f32[144,256]{1,0:T(8,128)S(1)}, f32[144,256]{1,0:T(8,128)}, u32[]{:S(2)}) copy-start(f32[144,256]{1,0:T(8,128)} %get-tuple-element.13) | copy-start | bytes 442372
  74.8 3.0 %copy-start.1 = (f32[48,256]{1,0:T(8,128)S(1)}, f32[48,256]{1,0:T(8,128)}, u32[]{:S(2)}) copy-start(f32[48,256]{1,0:T(8,128)} %get-tuple-element.14) | copy-start | bytes 147460

commit v2 on v1

--- a/solution.py
+++ b/solution.py
@@ -10,7 +10,6 @@
 
 F32, BF16 = jnp.float32, jnp.bfloat16
 CHUNKS = 4
-LAG = 4
 
 
 def dot(a, b):
@@ -22,15 +21,12 @@
 
 
 def kernel(
-    n, cells, cols, chans, fused, g_scale,
+    n, cells, cols, chans,
     x_hbm, cot_hbm, sw_hbm, tw_hbm, *rest,
 ):
-    if fused:
-        out_hbm, sg_hbm, tg_hbm = rest[:3]
-    else:
-        out_hbm, sg_hbm, tg_hbm = rest[:3]
+    out_hbm, sg_hbm, tg_hbm = rest[:3]
     (cotp, sw, tw, xs, vgs, agrad, act_t, x_t, s_sum, t_sum, out_v,
-     local_sem, out_sem, xsend, xfwd, xrecv, vsend, vfwd, vrecv) = rest[3:22]
+     local_sem, out_sem, xsend, xfwd, xrecv, vsend, vfwd, vrecv) = rest[3:]
     me = lax.axis_index("ta")
     core = lax.rem(me, 2)
     even = core == 0
@@ -46,8 +42,6 @@
         )
 
     steps = [1, 2, n - 1, n - 2]
-    if fused:
-        steps += [4, 8, 12]
     barrier = pltpu.get_barrier_semaphore()
     for step in steps:
         pl.semaphore_signal(
@@ -180,10 +174,6 @@
         vg = (agrad[at] * s * (1.0 + v * (1.0 - s))).astype(BF16)
         vgs[0, at] = vg
         act_t[...] = (v * s).astype(BF16).T
-        if LAG < CHUNKS:
-            @pl.when(k >= LAG)
-            def _():
-                send_v(k - LAG)
         for tap in range(3):
             x_t[tap * chans : (tap + 1) * chans] = xs[tap, at].T
         t_sum[...] += dot(x_t[...], vgs[0, at])
@@ -194,7 +184,7 @@
         return carry
 
     lax.fori_loop(0, CHUNKS, forward, 0)
-    for k in range(max(CHUNKS - LAG, 0), CHUNKS):
+    for k in range(CHUNKS):
         send_v(k)
 
     def back(k):
@@ -218,82 +208,12 @@
         out_v[at] = (cot + total).astype(BF16)
         pltpu.make_async_copy(out_v.at[at], out_hbm.at[at], out_sem.at[k]).start()
 
-    if fused:
-        (send1, recv1, send2, recv2, send3, recv3, sg, tg,
-         sem1, rsem1, sem2, rsem2, sem3, rsem3) = rest[22:]
-        z = me // 4
-        y = lax.rem(me // 2, 2)
-        sr = 9 * chans // n
-        tr = 3 * chans // n
-
-        def own(b):
-            return (s_sum[pl.ds(pl.multiple_of(sr * b, 16), sr)],
-                    t_sum[pl.ds(pl.multiple_of(tr * b, 16), tr)])
-
-        stage1 = []
-        for part in range(2):
-            to_y = 1 - y if part == 0 else y
-            for zz in range(4):
-                a, b = own(4 * zz + 2 * to_y + (1 - core))
-                send1[part, zz, 0:sr] = a.astype(BF16)
-                send1[part, zz, sr : sr + tr] = b.astype(BF16)
-            copy = remote(send1.at[part], recv1.at[part], sem1.at[part], rsem1.at[part],
-                          me + 1 - 2 * core)
-            copy.start()
-            stage1.append(copy)
-        stage1[0].wait_recv()
-        for zz in range(4):
-            a, b = own(4 * zz + 2 * (1 - y) + core)
-            send2[zz, 0:sr] = (a + recv1[0, zz, 0:sr].astype(F32)).astype(BF16)
-            send2[zz, sr : sr + tr] = (b + recv1[0, zz, sr : sr + tr].astype(F32)).astype(BF16)
-        stage2 = remote(send2, recv2, sem2.at[0], rsem2.at[0], me + 2 - 4 * y)
-        stage2.start()
-        half = CHUNKS // 2
-        for k in range(half):
-            back(k)
-        stage1[1].wait_recv()
-        stage2.wait_recv()
-
-        def sum2(zz):
-            a, b = own(4 * zz + 2 * y + core)
-            a = a + recv1[1, zz, 0:sr].astype(F32) + recv2[zz, 0:sr].astype(F32)
-            b = (b + recv1[1, zz, sr : sr + tr].astype(F32)
-                 + recv2[zz, sr : sr + tr].astype(F32))
-            return a, b
-
-        stage3 = []
-        for dz in (2, 1, 3):
-            zz = lax.rem(z + dz, 4)
-            a, b = sum2(zz)
-            send3[dz - 1, 0:sr] = a.astype(BF16)
-            send3[dz - 1, sr : sr + tr] = b.astype(BF16)
-            copy = remote(send3.at[dz - 1], recv3.at[dz - 1], sem3.at[dz - 1], rsem3.at[dz - 1],
-                          lax.rem(me + 4 * dz, n))
-            copy.start()
-            stage3.append(copy)
-        for k in range(half, CHUNKS):
-            back(k)
-        a, b = sum2(z)
-        for copy in stage3:
-            copy.wait_recv()
-        for slot in range(3):
-            a = a + recv3[slot, 0:sr].astype(F32)
-            b = b + recv3[slot, sr : sr + tr].astype(F32)
-        sg[...] = a * g_scale
-        tg[...] = b * g_scale
-        ends = [pltpu.make_async_copy(sg, sg_hbm, local_sem.at[0]),
-                pltpu.make_async_copy(tg, tg_hbm, local_sem.at[1])]
-        for copy in ends:
-            copy.start()
-        for copy in stage1 + [stage2] + stage3:
-            copy.wait_send()
-    else:
-        ends = [pltpu.make_async_copy(s_sum, sg_hbm, local_sem.at[0]),
-                pltpu.make_async_copy(t_sum, tg_hbm, local_sem.at[1])]
-        for copy in ends:
-            copy.start()
-        for k in range(CHUNKS):
-            back(k)
+    ends = [pltpu.make_async_copy(s_sum, sg_hbm, local_sem.at[0]),
+            pltpu.make_async_copy(t_sum, tg_hbm, local_sem.at[1])]
+    for copy in ends:
+        copy.start()
+    for k in range(CHUNKS):
+        back(k)
 
     for k in range(CHUNKS):
         for has, copy in ((x_has_one, x_one), (x_has_two, x_two), (x_has_pass, x_pass),
@@ -306,12 +226,402 @@
         copy.wait()
 
 
+def plane_kernel(
+    n, cells, cols, chans, g_scale,
+    x_hbm, cot_hbm, sw_hbm, tw_hbm, out_hbm, sg_hbm, tg_hbm,
+    cotp, sw, tw, xs, vgs, agrad, act_t, x_t, s_sum, t_sum, out_v, cot_v, back_v, home_v,
+    send1, recv1, send2, recv2, send3, recv3, sg, tg,
+    local_sem, out_sem, xsend, xrecv, hsend, csend, crecv, rsend, rrecv, esend, erecv,
+    vsend, vrecv, bsend, brecv, sem1, rsem1, sem2, rsem2, sem3, rsem3,
+):
+    me = lax.axis_index("ta")
+    planes = n // 4
+    z, q = me // 4, lax.rem(me, 4)
+    y, core = q // 2, lax.rem(q, 2)
+    base = me - q
+    mate = me + 1 - 2 * core
+    size = cells // 4
+    deep = size + 2 * cols
+    inner = pl.ds(cols, size)
+
+    def rows(k):
+        return pl.ds(pl.multiple_of(k * size, size), size)
+
+    def near(s):
+        return 2 * y + lax.rem(core + s, 2)
+
+    def far(s):
+        return 2 * (1 - y) + lax.rem(core + s, 2)
+
+    def remote(src, dst, ssem, rsem, to):
+        return pltpu.make_async_remote_copy(
+            src_ref=src, dst_ref=dst, send_sem=ssem, recv_sem=rsem,
+            device_id={"ta": to}, device_id_type=pl.DeviceIdType.MESH,
+        )
+
+    partners = [mate, base + far(0), base + far(1)]
+    partners += [lax.rem(me + 4 * dz, n) for dz in range(1, planes)]
+    barrier = pltpu.get_barrier_semaphore()
+    for to in partners:
+        pl.semaphore_signal(
+            barrier, inc=1, device_id={"ta": to}, device_id_type=pl.DeviceIdType.MESH
+        )
+    has_top = q == 2
+    has_bottom = q == 1
+    row_above = pl.ds((cells // 2) - cols, cols)
+    row_below = pl.ds(cells // 2, cols)
+    loads = [
+        pltpu.make_async_copy(cot_hbm.at[rows(q)], cotp.at[1, q, inner], local_sem.at[0]),
+        pltpu.make_async_copy(sw_hbm, sw, local_sem.at[1]),
+        pltpu.make_async_copy(x_hbm.at[rows(q)], xs.at[2 + q], local_sem.at[2]),
+        pltpu.make_async_copy(tw_hbm, tw, local_sem.at[3]),
+        pltpu.make_async_copy(cot_hbm, cot_v, local_sem.at[4]),
+    ]
+    for load in loads:
+        load.start()
+    top = pltpu.make_async_copy(
+        cot_hbm.at[row_above], cotp.at[1, q, pl.ds(0, cols)], local_sem.at[5])
+    bottom = pltpu.make_async_copy(
+        cot_hbm.at[row_below], cotp.at[1, q, pl.ds(cols + size, cols)], local_sem.at[5])
+
+    @pl.when(has_top)
+    def _():
+        top.start()
+
+    @pl.when(has_bottom)
+    def _():
+        bottom.start()
+
+    pl.semaphore_wait(barrier, len(partners))
+
+    dests = [far(0), far(1), near(1)]
+
+    def x_send(slot, to):
+        return remote(x_hbm.at[rows(to)], xs.at[2 + q], xsend.at[slot], xrecv.at[2 + q], base + to)
+
+    def cot_send(slot, to):
+        return remote(cot_hbm.at[rows(to)], cotp.at[1, q, inner], csend.at[slot],
+                      crecv.at[q], base + to)
+
+    def top_send(f):
+        return remote(cot_hbm.at[row_above], cotp.at[1, f, pl.ds(0, cols)], rsend.at[0],
+                      rrecv.at[f], base + 2)
+
+    def bottom_send(f):
+        return remote(cot_hbm.at[row_below], cotp.at[1, f, pl.ds(cols + size, cols)],
+                      rsend.at[1], rrecv.at[f], base + 1)
+
+    def edge_down(f):
+        return remote(cotp.at[1, f, pl.ds(size, cols)], cotp.at[1, f, pl.ds(0, cols)],
+                      esend.at[f], erecv.at[f], mate)
+
+    def edge_up(f):
+        return remote(cotp.at[1, f, pl.ds(cols, cols)], cotp.at[1, f, pl.ds(cols + size, cols)],
+                      esend.at[f], erecv.at[f], mate)
+
+    def x_halo(i):
+        return remote(xs.at[4 + i], xs.at[i], hsend.at[i], xrecv.at[i], lax.rem(me + 4, n))
+
+    def v_halo(i):
+        return remote(vgs.at[i], vgs.at[4 + i], vsend.at[i], vrecv.at[i],
+                      lax.rem(me + n - 4, n))
+
+    def b_send(f):
+        return remote(back_v.at[f], home_v.at[rows(q)], bsend.at[f], brecv.at[q], base + f)
+
+    for slot, to in enumerate(dests):
+        x_send(slot, to).start()
+    cot_send(2, dests[2]).start()
+
+    @pl.when(q != 2)
+    def _():
+        top_send(q).start()
+
+    @pl.when(q != 1)
+    def _():
+        bottom_send(q).start()
+
+    for slot in range(2):
+        cot_send(slot, dests[slot]).start()
+
+    none = jnp.zeros((size, chans), BF16)
+    edge = jnp.zeros((cols, chans), BF16)
+
+    @pl.when(z == 0)
+    def _():
+        xs[0] = none
+        xs[1] = none
+
+    @pl.when(z == planes - 1)
+    def _():
+        vgs[4] = none
+        vgs[5] = none
+
+    @pl.when(q == 0)
+    def _():
+        for f in range(4):
+            cotp[1, f, pl.ds(0, cols)] = edge
+
+    @pl.when(q == 3)
+    def _():
+        for f in range(4):
+            cotp[1, f, pl.ds(cols + size, cols)] = edge
+
+    loads[2].wait()
+
+    def pass_frames():
+        for f in (2, 3):
+            @pl.when(q != f)
+            def _():
+                remote(xs.at[2 + f], xs.at[2 + f], xsend.at[0], xrecv.at[2 + f], mate).wait_recv()
+
+            @pl.when(z < planes - 1)
+            def _():
+                x_halo(f - 2).start()
+
+    @pl.when(y == 1)
+    def _():
+        pass_frames()
+
+    def trade_edges(f):
+        @pl.when(core == 0)
+        def _():
+            edge_down(f).start()
+
+        @pl.when(core == 1)
+        def _():
+            edge_up(f).start()
+
+    def cot_arrives(f):
+        remote(cotp.at[1, f, inner], cotp.at[1, f, inner], csend.at[0], crecv.at[f],
+               mate).wait_recv()
+
+    def shift(f):
+        edge_down(f).wait_recv()
+        piece = cotp[1, f].astype(F32)
+        col = lax.rem(lax.broadcasted_iota(jnp.int32, (deep, chans), 0), cols)
+        cotp[0, f] = jnp.where(col == cols - 1, 0.0, pltpu.roll(piece, deep - 1, 0)).astype(BF16)
+        cotp[2, f] = jnp.where(col == 0, 0.0, pltpu.roll(piece, 1, 0)).astype(BF16)
+
+    def cot_at(f, i, j):
+        return cotp[j, f, pl.ds((2 - i) * cols, size)]
+
+    def adjoint(f):
+        total = jnp.zeros((size, chans), F32)
+        for i in range(3):
+            for j in range(3):
+                total = total + dot_t(cot_at(f, i, j), sw[i, j])
+        agrad[f] = total
+
+    def cross_row(f):
+        @pl.when(jnp.logical_or(has_top, has_bottom))
+        def _():
+            top_send(f).wait_recv()
+
+    loads[0].wait()
+    trade_edges(q)
+    cot_arrives(near(1))
+    trade_edges(near(1))
+
+    @pl.when(has_top)
+    def _():
+        top.wait()
+
+    @pl.when(has_bottom)
+    def _():
+        bottom.wait()
+
+    cross_row(near(1))
+    loads[1].wait()
+    s_sum[...] = jnp.zeros_like(s_sum)
+    t_sum[...] = jnp.zeros_like(t_sum)
+
+    def local_adjoint(s, carry):
+        shift(near(s))
+        adjoint(near(s))
+        return carry
+
+    lax.fori_loop(0, 2, local_adjoint, 0)
+
+    @pl.when(y == 0)
+    def _():
+        pass_frames()
+
+    for f in (0, 1):
+        @pl.when(q != f)
+        def _():
+            remote(xs.at[2 + f], xs.at[2 + f], xsend.at[0], xrecv.at[2 + f], mate).wait_recv()
+    loads[3].wait()
+
+    @pl.when(z > 0)
+    def _():
+        for i in range(2):
+            x_halo(i).wait_recv()
+
+    def forward(f):
+        v = dot(xs[2 + f], tw[0]) + dot(xs[1 + f], tw[1]) + dot(xs[f], tw[2])
+        s = 1.0 / (1.0 + jnp.exp(-v))
+        vg = (agrad[f] * s * (1.0 + v * (1.0 - s))).astype(BF16)
+        vgs[f] = vg
+
+        @pl.when(jnp.logical_and(z > 0, f < 2))
+        def _():
+            v_halo(f).start()
+
+        act_t[...] = (v * s).astype(BF16).T
+        for tap in range(3):
+            x_t[tap * chans : (tap + 1) * chans] = xs[2 + f - tap].T
+        t_sum[...] += dot(x_t[...], vgs[f])
+        for i in range(3):
+            for j in range(3):
+                block = pl.ds((3 * i + j) * chans, chans)
+                s_sum[block] += dot(act_t[...], cot_at(f, i, j))
+
+    def local_forward(s, carry):
+        forward(near(s))
+        return carry
+
+    lax.fori_loop(0, 2, local_forward, 0)
+    for s in range(2):
+        cot_arrives(far(s))
+        trade_edges(far(s))
+        cross_row(far(s))
+
+    def far_forward(s, carry):
+        shift(far(s))
+        adjoint(far(s))
+        forward(far(s))
+        return carry
+
+    lax.fori_loop(0, 2, far_forward, 0)
+
+    def back(f):
+        total = dot_t(vgs[f], tw[0]) + dot_t(vgs[f + 1], tw[1]) + dot_t(vgs[f + 2], tw[2])
+        back_v[f] = total.astype(BF16)
+
+        @pl.when(q == f)
+        def _():
+            home_v[rows(q)] = back_v[f]
+
+        @pl.when(q != f)
+        def _():
+            b_send(f).start()
+
+    sr = 9 * chans // n
+    tr = 3 * chans // n
+
+    def own(b):
+        return (s_sum[pl.ds(pl.multiple_of(sr * b, 16), sr)],
+                t_sum[pl.ds(pl.multiple_of(tr * b, 16), tr)])
+
+    stage1 = []
+    for part in range(2):
+        to_y = 1 - y if part == 0 else y
+        for zz in range(4):
+            a, b = own(4 * zz + 2 * to_y + (1 - core))
+            send1[part, zz, 0:sr] = a.astype(BF16)
+            send1[part, zz, sr : sr + tr] = b.astype(BF16)
+        copy = remote(send1.at[part], recv1.at[part], sem1.at[part], rsem1.at[part],
+                      me + 1 - 2 * core)
+        copy.start()
+        stage1.append(copy)
+    back(0)
+    back(1)
+    stage1[0].wait_recv()
+    for zz in range(4):
+        a, b = own(4 * zz + 2 * (1 - y) + core)
+        send2[zz, 0:sr] = (a + recv1[0, zz, 0:sr].astype(F32)).astype(BF16)
+        send2[zz, sr : sr + tr] = (b + recv1[0, zz, sr : sr + tr].astype(F32)).astype(BF16)
+    stage2 = remote(send2, recv2, sem2.at[0], rsem2.at[0], me + 2 - 4 * y)
+    stage2.start()
+    for f in (2, 3):
+        @pl.when(z < planes - 1)
+        def _():
+            v_halo(f - 2).wait_recv()
+
+        back(f)
+    stage1[1].wait_recv()
+    stage2.wait_recv()
+
+    def sum2(zz):
+        a, b = own(4 * zz + 2 * y + core)
+        a = a + recv1[1, zz, 0:sr].astype(F32) + recv2[zz, 0:sr].astype(F32)
+        b = (b + recv1[1, zz, sr : sr + tr].astype(F32)
+             + recv2[zz, sr : sr + tr].astype(F32))
+        return a, b
+
+    stage3 = []
+    for dz in (2, 1, 3):
+        zz = lax.rem(z + dz, planes)
+        a, b = sum2(zz)
+        send3[dz - 1, 0:sr] = a.astype(BF16)
+        send3[dz - 1, sr : sr + tr] = b.astype(BF16)
+        copy = remote(send3.at[dz - 1], recv3.at[dz - 1], sem3.at[dz - 1], rsem3.at[dz - 1],
+                      lax.rem(me + 4 * dz, n))
+        copy.start()
+        stage3.append(copy)
+    loads[4].wait()
+    for r in range(4):
+        @pl.when(q != r)
+        def _():
+            remote(home_v.at[rows(r)], home_v.at[rows(r)], bsend.at[0], brecv.at[r],
+                   mate).wait_recv()
+
+        at = rows(r)
+        out_v[at] = (cot_v[at].astype(F32) + home_v[at].astype(F32)).astype(BF16)
+        pltpu.make_async_copy(out_v.at[at], out_hbm.at[at], out_sem.at[r]).start()
+    a, b = sum2(z)
+    for copy in stage3:
+        copy.wait_recv()
+    for slot in range(3):
+        a = a + recv3[slot, 0:sr].astype(F32)
+        b = b + recv3[slot, sr : sr + tr].astype(F32)
+    sg[...] = a * g_scale
+    tg[...] = b * g_scale
+    ends = [pltpu.make_async_copy(sg, sg_hbm, local_sem.at[0]),
+            pltpu.make_async_copy(tg, tg_hbm, local_sem.at[1])]
+    for copy in ends:
+        copy.start()
+    for copy in stage1 + [stage2] + stage3:
+        copy.wait_send()
+    for slot, to in enumerate(dests):
+        x_send(slot, to).wait_send()
+        cot_send(slot, to).wait_send()
+
+    @pl.when(q != 2)
+    def _():
+        top_send(q).wait_send()
+
+    @pl.when(q != 1)
+    def _():
+        bottom_send(q).wait_send()
+
+    for i in range(2):
+        @pl.when(z < planes - 1)
+        def _():
+            x_halo(i).wait_send()
+
+        @pl.when(z > 0)
+        def _():
+            v_halo(i).wait_send()
+    for f in range(4):
+        edge_down(f).wait_send()
+
+        @pl.when(q != f)
+        def _():
+            b_send(f).wait_send()
+
+        pltpu.make_async_copy(out_v.at[rows(f)], out_hbm.at[rows(f)], out_sem.at[f]).wait()
+    for copy in ends:
+        copy.wait()
+
+
 def body(n, frames_in, cotangent, spatial_w, temporal_w):
     resident, height, cols, chans = frames_in.shape
     cells = resident * height * cols
     g_scale = 1.0 / math.sqrt(n * cells)
     sr, tr = 9 * chans // n, 3 * chans // n
-    fused = n == 16 and sr % 16 == 0 and tr % 16 == 0
+    fused = n == 16 and resident == 1 and height % 4 == 0 and sr % 16 == 0 and tr % 16 == 0
     both = sr + tr
     dma = pltpu.SemaphoreType.DMA
     scratch = [
@@ -331,18 +641,37 @@
         dma((2, CHUNKS)), dma((CHUNKS,)), dma((2, CHUNKS)),
     ]
     if fused:
-        scratch += [
+        size = cells // 4
+        scratch = [
+            pltpu.VMEM((3, 4, size + 2 * cols, chans), BF16),
+            pltpu.VMEM((3, 3, chans, chans), BF16),
+            pltpu.VMEM((3, chans, chans), BF16),
+            pltpu.VMEM((6, size, chans), BF16),
+            pltpu.VMEM((6, size, chans), BF16),
+            pltpu.VMEM((4, size, chans), F32),
+            pltpu.VMEM((chans, size), BF16),
+            pltpu.VMEM((3 * chans, size), BF16),
+            pltpu.VMEM((9 * chans, chans), F32),
+            pltpu.VMEM((3 * chans, chans), F32),
+            pltpu.VMEM((cells, chans), BF16),
+            pltpu.VMEM((cells, chans), BF16),
+            pltpu.VMEM((4, size, chans), BF16),
+            pltpu.VMEM((cells, chans), BF16),
             pltpu.VMEM((2, 4, both, chans), BF16), pltpu.VMEM((2, 4, both, chans), BF16),
             pltpu.VMEM((4, both, chans), BF16), pltpu.VMEM((4, both, chans), BF16),
             pltpu.VMEM((3, both, chans), BF16), pltpu.VMEM((3, both, chans), BF16),
             pltpu.VMEM((sr, chans), F32), pltpu.VMEM((tr, chans), F32),
+            dma((6,)), dma((4,)), dma((3,)), dma((6,)), dma((2,)), dma((3,)), dma((4,)),
+            dma((2,)), dma((4,)), dma((4,)), dma((4,)), dma((2,)), dma((2,)), dma((4,)), dma((4,)),
             dma((2,)), dma((2,)), dma((1,)), dma((1,)), dma((3,)), dma((3,)),
         ]
+        step = functools.partial(plane_kernel, n, cells, cols, chans, g_scale)
     else:
         sr, tr = 9 * chans, 3 * chans
+        step = functools.partial(kernel, n, cells, cols, chans)
     anywhere = pl.BlockSpec(memory_space=pl.ANY)
     input_grad, sg, tg = pl.pallas_call(
-        functools.partial(kernel, n, cells, cols, chans, fused, g_scale),
+        step,
         out_shape=(
             jax.ShapeDtypeStruct((cells, chans), BF16),
             jax.ShapeDtypeStruct((sr, chans), F32),
@@ -352,7 +681,7 @@
         out_specs=(anywhere,) * 3,
         scratch_shapes=scratch,
         compiler_params=pltpu.CompilerParams(
-            collective_id=0, has_side_effects=True, vmem_limit_bytes=56 * 1024 * 1024
+            collective_id=0 if fused else 1, has_side_effects=True, vmem_limit_bytes=56 * 1024 * 1024
         ),
     )(frames_in.reshape(cells, chans), cotangent.reshape(cells, chans), spatial_w, temporal_w)
     if not fused:

time: 78.6 us -> 73.8 us (0.939)
  Pallas kernels: 74.1 us -> 69.4 us
    pallas_call x1, Pallas kernels: 74.1 us -> 69.4 us  [body(): pl.pallas_call(step, out_shape=(jax.ShapeDtypeStruct((cells, chans), BF16...]
where the time goes in v2:
time: 73.8 us; the launch traced here: 73.7 us
  Pallas kernels  69.4 us (94%)
  local copies, waits for them, and re-layouts  3.61 us (5%)
    pallas_call x1, Pallas kernels, body(): pl.pallas_call(step, out_shape=(jax.ShapeDtypeStruct((cells, chans), BF16...  69.4 us
    unnamed x7, local copies, waits for them, and re-layouts  3.61 us

profile of v2, /device:TPU:0, one launch (start us, length us, event | category | flops | bytes accessed | tf_op | source)
XLA Modules:
  0.0 73.7 jit_solution(13972251098926070011)
XLA Ops:
  0.6 69.4 %shard_map.67 = (bf16[2048,256]{1,0:T(8,128)(2,1)}, f32[144,256]{1,0:T(8,128)}, f32[48,256]{1,0:T(8,128)}) custom-call(bf16[2048,256]{1,0:T(8,128)(2,1)} %bitcast.3, bf16[2048,256]{1,0:T(8,128)(2,1)} %bitcast.4, bf16[3,3,256,256]{3,2,1,0:T(8,128)(2,1)} %sw_hbm.1, bf16[3,256,256]{2,1,0:T(8,128)(2,1)} %tw_hbm.1), custom_call_target="tpu_custom_call" | custom-call | tf_op jit(solution)/shard_map/pallas_call | solution.py:673
  70.0 0.0 copy-start
  70.1 0.0 copy-start.1
  70.1 2.3 %copy.10 = bf16[1,16,128,256]{3,2,1,0:T(8,128)(2,1)} copy(bf16[1,16,128,256]{3,2,1,0:T(8,128)(2,1)} %bitcast.5) | data formatting | bytes 2097152
  72.4 0.0 copy-done
  72.4 0.7 copy.11
  73.1 0.0 copy-done.1
  73.1 0.6 copy.12
Async XLA Ops:
  70.0 2.3 %copy-start = (f32[144,256]{1,0:T(8,128)S(1)}, f32[144,256]{1,0:T(8,128)}, u32[]{:S(2)}) copy-start(f32[144,256]{1,0:T(8,128)} %get-tuple-element.13) | copy-start | bytes 442372
  70.1 3.0 %copy-start.1 = (f32[48,256]{1,0:T(8,128)S(1)}, f32[48,256]{1,0:T(8,128)}, u32[]{:S(2)}) copy-start(f32[48,256]{1,0:T(8,128)} %get-tuple-element.14) | copy-start | bytes 147460

commit v3 on v2

--- a/solution.py
+++ b/solution.py
@@ -525,8 +525,6 @@
                       me + 1 - 2 * core)
         copy.start()
         stage1.append(copy)
-    back(0)
-    back(1)
     stage1[0].wait_recv()
     for zz in range(4):
         a, b = own(4 * zz + 2 * (1 - y) + core)
@@ -534,6 +532,8 @@
         send2[zz, sr : sr + tr] = (b + recv1[0, zz, sr : sr + tr].astype(F32)).astype(BF16)
     stage2 = remote(send2, recv2, sem2.at[0], rsem2.at[0], me + 2 - 4 * y)
     stage2.start()
+    back(0)
+    back(1)
     for f in (2, 3):
         @pl.when(z < planes - 1)
         def _():

time: 73.8 us -> 65.2 us (0.88)
  the two profiles are of different devices: /device:TPU:0 before, /device:TPU:1 now
where the time goes in v3:
time: 65.2 us; the launch traced here: 65 us
  Pallas kernels  60.8 us (93%)
  local copies, waits for them, and re-layouts  3.61 us (6%)
  between operations  0.66 us (1%)
    pallas_call x1, Pallas kernels, body(): pl.pallas_call(step, out_shape=(jax.ShapeDtypeStruct((cells, chans), BF16...  60.8 us
    unnamed x7, local copies, waits for them, and re-layouts  3.61 us

profile of v3, /device:TPU:1, one launch (start us, length us, event | category | flops | bytes accessed | tf_op | source)
XLA Modules:
  0.0 65.0 jit_solution(17341061980089298031)
XLA Ops:
  0.6 60.8 %shard_map.67 = (bf16[2048,256]{1,0:T(8,128)(2,1)}, f32[144,256]{1,0:T(8,128)}, f32[48,256]{1,0:T(8,128)}) custom-call(bf16[2048,256]{1,0:T(8,128)(2,1)} %bitcast.3, bf16[2048,256]{1,0:T(8,128)(2,1)} %bitcast.4, bf16[3,3,256,256]{3,2,1,0:T(8,128)(2,1)} %sw_hbm.1, bf16[3,256,256]{2,1,0:T(8,128)(2,1)} %tw_hbm.1), custom_call_target="tpu_custom_call" | custom-call | tf_op jit(solution)/shard_map/pallas_call | solution.py:673
  61.4 0.0 copy-start
  61.4 0.0 copy-start.1
  61.4 2.3 %copy.10 = bf16[1,16,128,256]{3,2,1,0:T(8,128)(2,1)} copy(bf16[1,16,128,256]{3,2,1,0:T(8,128)(2,1)} %bitcast.5) | data formatting | bytes 2097152
  63.7 0.0 copy-done
  63.7 0.7 %copy.11 = f32[144,256]{1,0:T(8,128)} copy(f32[144,256]{1,0:T(8,128)S(1)} %copy-done) | data formatting | bytes 294912
  64.4 0.0 copy-done.1
  64.4 0.6 copy.12
Async XLA Ops:
  61.4 2.3 %copy-start = (f32[144,256]{1,0:T(8,128)S(1)}, f32[144,256]{1,0:T(8,128)}, u32[]{:S(2)}) copy-start(f32[144,256]{1,0:T(8,128)} %get-tuple-element.13) | copy-start | bytes 442372
  61.4 3.0 %copy-start.1 = (f32[48,256]{1,0:T(8,128)S(1)}, f32[48,256]{1,0:T(8,128)}, u32[]{:S(2)}) copy-start(f32[48,256]{1,0:T(8,128)} %get-tuple-element.14) | copy-start | bytes 147460
